TPU v7x, 512 devices: a whole 4x8x8 slice. The times are simulated.
512 devices in a mesh: mem: 8 (over x, core), col: 64 (over z, y).
Axes of the slice: x: 4, y: 8, z: 8, core: 2. Of those that a mesh axis runs over, the one named last changes fastest.
Arguments:
- ensemble: bfloat16 [80, 512, 1024], P('mem', 'col'), may hold values from -6 to 6
- obs_prior: float32 [80, 16384], P(None, 'col'), may hold values from -6 to 6
- obs_value: float32 [16384], P('col'), may hold values from -8 to 8
- obs_var: float32 [16384], P('col'), may hold values from 0.25 to 4
- obs_noise: float32 [80, 16384], P(None, 'col'), may hold values from -6 to 6
- obs_block: int32 [16384], P('col'), may hold values from 0 to 511
- batch_owner: int32 [8], replicated, may hold values from 0 to 63, as said below
Outputs:
- analysis: bfloat16 [80, 512, 1024], P('mem', 'col')
- obs_posterior: float32 [80, 16384], P(None, 'col')
Inputs may be any that keep to these rules, and one draw needn't show every extreme that they name: `batch_owner`: the 8 entries are distinct; both 0 and 63 occur.
All inputs are finite; a program needn't handle non-finite values.
Results may differ from a plain program's by a relative error of at most 0.001.
Values may be sent and summed in bfloat16 or wider, within the bound.
A program may use at most 128 MiB of HBM per device.

v0:
```python
import math

import jax
import jax.numpy as jnp
from jax import lax
from jax.sharding import PartitionSpec as P

BLK_DEV = 8


highest = lax.Precision.HIGHEST


def from_root(value, axis, source):
    kept = jnp.where(lax.axis_index(axis) == source, value, 0).astype(value.dtype)
    return lax.psum(kept, axis)


def taper(offset, blocks):
    cosine = jnp.cos(offset * (math.pi / blocks))
    square = cosine * cosine
    fourth = square * square
    return fourth * fourth


def batch_factors(priors_now, perturbed, variance, position, blocks):
    members = priors_now.shape[0]
    spread = priors_now - jnp.mean(priors_now, axis=0, keepdims=True)
    covariance = jnp.dot(
        spread.T, spread, precision=highest, preferred_element_type=jnp.float32
    ) / (members - 1)
    system = taper(position[:, None] - position[None, :], blocks) * covariance + jnp.diag(variance)
    factor_low = jnp.linalg.cholesky(system)
    solved = jax.scipy.linalg.cho_solve((factor_low, True), (perturbed - priors_now).T)
    return (spread, solved)


def regress(values_in, spread, solved, weight):
    members = values_in.shape[0]
    anomaly = values_in - jnp.mean(values_in, axis=0, keepdims=True)
    covariance = jnp.dot(
        spread.T, anomaly, precision=highest, preferred_element_type=jnp.float32
    ) / (members - 1)
    return values_in + jnp.dot(
        solved.T, weight * covariance, precision=highest, preferred_element_type=jnp.float32
    )


def shards(ensemble, obs_prior, obs_value, obs_var, obs_noise, obs_block, batch_owner):
    columns_n = lax.axis_size("col")
    column = lax.axis_index("col")
    blocks = BLK_DEV * columns_n
    perturbed_own = obs_value[None, :] + jnp.sqrt(obs_var)[None, :] * obs_noise
    position_own = obs_block.astype(jnp.float32)
    obs_pool = obs_prior
    batch_total = batch_owner.shape[0]
    factors = []
    for batch_number in range(batch_total):
        priors_now, perturbed, variance, position = (
            from_root(obs_pool, "col", batch_owner[batch_number]),
            from_root(perturbed_own, "col", batch_owner[batch_number]),
            from_root(obs_var, "col", batch_owner[batch_number]),
            from_root(position_own, "col", batch_owner[batch_number]),
        )
        spread, solved = batch_factors(priors_now, perturbed, variance, position, blocks)
        obs_pool = regress(
            obs_pool, spread, solved, taper(position[:, None] - position_own[None, :], blocks)
        )
        factors.append((spread, solved, position))
    members_slab = lax.all_to_all(ensemble, "mem", split_axis=2, concat_axis=0, tiled=True)
    first_block = column * BLK_DEV
    members, blocks_held, cells_held = members_slab.shape
    block_ids = (first_block + jnp.arange(blocks_held, dtype=jnp.int32)).astype(jnp.float32)
    state_cols = members_slab.astype(jnp.float32)
    segment_len = math.gcd(cells_held, 1024)
    segments_per = cells_held // segment_len
    segments = state_cols.transpose(1, 0, 2)
    segment_ids = jnp.repeat(block_ids, segments_per)

    def advance(segment_args):
        segment, block_id = segment_args
        for spread, solved, position in factors:
            segment = regress(segment, spread, solved, taper(block_id - position, blocks)[:, None])
        return segment

    finished = lax.map(advance, (segments, segment_ids))
    updated = finished.transpose(1, 0, 2)
    rounded = updated.astype(jnp.bfloat16)
    analysis = lax.all_to_all(rounded, "mem", split_axis=0, concat_axis=2, tiled=True)
    return (analysis, obs_pool)


def solution(mesh):
    return jax.shard_map(
        shards,
        mesh=mesh,
        in_specs=(
            P("mem", "col", None),
            P(None, "col"),
            P("col"),
            P("col"),
            P(None, "col"),
            P("col"),
            P(),
        ),
        out_specs=(P("mem", "col", None), P(None, "col")),
        check_vma=False,
    )
```

profile of v0, /device:TPU:1, one launch (start us, length us, event | category | flops | bytes accessed | tf_op | source)
XLA Modules:
  0.0 2011.9 jit_solution(6820243528962553385)
XLA Ops:
  31.1 226.7 %all-reduce.1 = (f32[256]{0:T(256)S(1)}, f32[256]{0:T(256)S(1)}, f32[256]{0:T(256)S(1)}, f32[256]{0:T(256)S(1)}, f32[256]{0:T(256)S(1)}, /*index=5*/f32[256]{0:T...) all-reduce(f32[256]{0:T(256)S(1)} %get-tuple-element.645, ...), channel_id=1, replica_groups=mesh['mem'=8,'col'=64] {'col'}, use_global_device_ids=true, to_apply=%region_0.1 | all-reduce | flops 4096 | bytes 32768 | tf_op jit(solution)/shard_map/psum | solution.py:16
  308.9 30.7 %custom-call.28 = f32[2,128,128]{1,2,0:T(8,128)S(1)} custom-call(f32[2,128,128]{2,1,0:T(8,128)S(1)} %get-tuple-element.197), custom_call_target="InvertDiagBlocksLowerTriangular" | custom-call | tf_op jit(solution)/shard_map/jit(_cho_solve)/triangular_solve | solution.py:34
  343.5 193.2 %all-reduce.31.cloned.1.call-done = (f32[80,256]{1,0:T(8,128)}, f32[80,256]{1,0:T(8,128)}) async-done(((f32[80,256]{1,0:T(8,128)}, f32[80,256]{1,0:T(8,128)}), (f32[80,256]{1,0:T(8,128)}, f32[80,256]{1,0:T(8,128)})) %all-reduce.31.cloned.1.call-update) | async-done | bytes 163856 | tf_op jit(solution)/shard_map/psum | solution.py:16
  562.2 11.7 cholesky.433
  581.1 19.7 custom-call.30
  604.8 147.4 %all-reduce.29.cloned.1.call-done = (f32[80,256]{1,0:T(8,128)}, f32[80,256]{1,0:T(8,128)}) async-done(((f32[80,256]{1,0:T(8,128)}, f32[80,256]{1,0:T(8,128)}), (f32[80,256]{1,0:T(8,128)}, f32[80,256]{1,0:T(8,128)})) %all-reduce.29.cloned.1.call-update) | async-done | bytes 163856 | tf_op jit(solution)/shard_map/psum | solution.py:16
  777.5 11.7 cholesky.467
  796.2 19.7 custom-call.32
  819.9 147.3 %all-reduce.27.cloned.1.call-done = (f32[80,256]{1,0:T(8,128)}, f32[80,256]{1,0:T(8,128)}) async-done(((f32[80,256]{1,0:T(8,128)}, f32[80,256]{1,0:T(8,128)}), (f32[80,256]{1,0:T(8,128)}, f32[80,256]{1,0:T(8,128)})) %all-reduce.27.cloned.1.call-update) | async-done | bytes 163856 | tf_op jit(solution)/shard_map/psum | solution.py:16
  992.7 11.7 cholesky.501
  1011.6 19.7 custom-call.34
  1035.2 147.3 %all-reduce.25.cloned.1.call-done = (f32[80,256]{1,0:T(8,128)}, f32[80,256]{1,0:T(8,128)}) async-done(((f32[80,256]{1,0:T(8,128)}, f32[80,256]{1,0:T(8,128)}), (f32[80,256]{1,0:T(8,128)}, f32[80,256]{1,0:T(8,128)})) %all-reduce.25.cloned.1.call-update) | async-done | bytes 163856 | tf_op jit(solution)/shard_map/psum | solution.py:16
  1208.0 11.7 cholesky.535
  1226.6 19.7 custom-call.36
  1250.3 147.4 %all-reduce.23.cloned.1.call-done = (f32[80,256]{1,0:T(8,128)}, f32[80,256]{1,0:T(8,128)}) async-done(((f32[80,256]{1,0:T(8,128)}, f32[80,256]{1,0:T(8,128)}), (f32[80,256]{1,0:T(8,128)}, f32[80,256]{1,0:T(8,128)})) %all-reduce.23.cloned.1.call-update) | async-done | bytes 163856 | tf_op jit(solution)/shard_map/psum | solution.py:16
  1423.1 11.7 cholesky.569
  1442.0 19.7 custom-call.38
  1465.7 147.4 %all-reduce.21.cloned.1.call-done = (f32[80,256]{1,0:T(8,128)}, f32[80,256]{1,0:T(8,128)}) async-done(((f32[80,256]{1,0:T(8,128)}, f32[80,256]{1,0:T(8,128)}), (f32[80,256]{1,0:T(8,128)}, f32[80,256]{1,0:T(8,128)})) %all-reduce.21.cloned.1.call-update) | async-done | bytes 163856 | tf_op jit(solution)/shard_map/psum | solution.py:16
  1638.5 11.7 cholesky.603
  1657.2 19.7 custom-call.40
  1680.8 147.4 %all-reduce.19.cloned.1.call-done = (f32[80,256]{1,0:T(8,128)}, f32[80,256]{1,0:T(8,128)}) async-done(((f32[80,256]{1,0:T(8,128)}, f32[80,256]{1,0:T(8,128)}), (f32[80,256]{1,0:T(8,128)}, f32[80,256]{1,0:T(8,128)})) %all-reduce.19.cloned.1.call-update) | async-done | bytes 163856 | tf_op jit(solution)/shard_map/psum | solution.py:16
  1853.6 11.7 cholesky.637
  1872.3 19.9 custom-call.42
  1893.6 95.8 %while.26 = (s32[]{:T(128)}, bf16[8,80,128]{2,0,1:T(8,128)(2,1)}, f32[8,80,128]{2,0,1:T(8,128)S(1)}, f32[80,256]{1,0:T(8,128)S(1)}, f32[8]{0:T(128)S(1)}, /*inde...) while((s32[]{:T(128)}, bf16[8,80,128]{2,0,1:T(8,128)(2,1)}, ...), condition=%wide.region_60.63_spmd, body=%wide.region_51.62_spmd.sunk | while | flops 503836672 | bytes 4636989 | solution.py:86
  (595 shorter events, 457.2 us)
Async XLA Ops:
  7.2 17.2 copy-start.2
  7.2 22.8 %copy-start.4 = (f32[256]{0:T(256)S(1)}, f32[256]{0:T(256)}, u32[]{:S(2)}) copy-start(f32[256]{0:T(256)} %param.15) | copy-start | bytes 3076
  7.2 22.9 %copy-start.1 = (f32[80,256]{1,0:T(8,128)S(1)}, f32[80,256]{1,0:T(8,128)}, u32[]{:S(2)}) copy-start(f32[80,256]{1,0:T(8,128)} %param.16) | copy-start | bytes 245764
  7.2 22.9 %copy-start.5 = (f32[256]{0:T(256)S(1)}, f32[256]{0:T(256)}, u32[]{:S(2)}) copy-start(f32[256]{0:T(256)} %param.14) | copy-start | bytes 3076
  7.2 22.9 %copy-start = (f32[80,256]{1,0:T(8,128)S(1)}, f32[80,256]{1,0:T(8,128)}, u32[]{:S(2)}) copy-start(f32[80,256]{1,0:T(8,128)} %param.13) | copy-start | bytes 245764
  9.9 21.1 %copy-start.3 = (s32[256]{0:T(256)S(1)}, s32[256]{0:T(256)}, u32[]{:S(2)}) copy-start(s32[256]{0:T(256)} %param.17) | copy-start | bytes 3076
  14.2 243.7 %all-to-all-start = ((bf16[8,2,5120]{2,1,0:T(2,128)(2,1)}), bf16[8,2,5120]{2,1,0:T(2,128)(2,1)S(1)}, u32[]{:S(2)}, u32[]{:S(2)}) async-start(bf16[8,2,5120]{2,1,0:T(2,128)(2,1)} %reshape.256), calls=%async_computation | async-start | bytes 327680 | tf_op jit(solution)/shard_map/all_to_all | solution.py:70
  24.3 240.6 %all-reduce.33.cloned.1.call-start = ((), (), s32[]{:S(2)}) async-start(), calls=%async_computation.9 | async-start | bytes 327680 | tf_op jit(solution)/shard_map/psum | solution.py:16
  31.0 505.8 %all-reduce.31.cloned.1.call-start = ((), (), s32[]{:S(2)}) async-start(), calls=%async_computation.8 | async-start | bytes 327680 | tf_op jit(solution)/shard_map/psum | solution.py:16
  343.5 408.6 %all-reduce.29.cloned.1.call-start = ((), (), s32[]{:S(2)}) async-start(), calls=%async_computation.7 | async-start | bytes 327680 | tf_op jit(solution)/shard_map/psum | solution.py:16
  604.7 362.5 %all-reduce.27.cloned.1.call-start = ((), (), s32[]{:S(2)}) async-start(), calls=%async_computation.6 | async-start | bytes 327680 | tf_op jit(solution)/shard_map/psum | solution.py:16
  819.8 362.7 %all-reduce.25.cloned.1.call-start = ((), (), s32[]{:S(2)}) async-start(), calls=%async_computation.5 | async-start | bytes 327680 | tf_op jit(solution)/shard_map/psum | solution.py:16
  1035.2 362.5 %all-reduce.23.cloned.1.call-start = ((), (), s32[]{:S(2)}) async-start(), calls=%async_computation.4 | async-start | bytes 327680 | tf_op jit(solution)/shard_map/psum | solution.py:16
  1250.3 362.8 %all-reduce.21.cloned.1.call-start = ((), (), s32[]{:S(2)}) async-start(), calls=%async_computation.3 | async-start | bytes 327680 | tf_op jit(solution)/shard_map/psum | solution.py:16
  1465.6 362.6 %all-reduce.19.cloned.1.call-start = ((), (), s32[]{:S(2)}) async-start(), calls=%async_computation.2 | async-start | bytes 327680 | tf_op jit(solution)/shard_map/psum | solution.py:16
  1989.4 14.7 all-to-all-start.1
Sparse Core Ops, SparseCore 0:
  31.1 147.5 all-reduce.32
  343.6 193.0 all-reduce.30
  604.8 147.2 all-reduce.28
  820.0 147.2 all-reduce.26
  1035.3 147.2 all-reduce.24
  1250.4 147.2 all-reduce.22
  1465.8 147.2 all-reduce.20
  1680.9 147.2 all-reduce.18
where the time goes:
time: 2020 us; the launch traced here: 2010 us
  waiting for transfers between devices  1080 us (53%)
  other arithmetic  485 us (24%)
  blocking collectives  227 us (11%)
  matrix products  89.2 us (4%)
  local copies, waits for them, and re-layouts  76.1 us (4%)
  between operations  31 us (2%)
    psum x8, waiting for transfers between devices, from_root(): return lax.psum(kept, axis)  1080 us
    another operation x56, other arithmetic, batch_factors(): factor_low = jnp.linalg.cholesky(system)  277 us
    psum x1, blocking collectives, from_root(): return lax.psum(kept, axis)  227 us
    another operation x25, other arithmetic, batch_factors(): jax.scipy.linalg.cho_solve((factor_low, True), (perturbed - priors_now).T)  169 us
  transfers between devices with their start and end apart: 10, of which 8 were waited for; matrix products, arithmetic and copies ran while one was open for 1% of the time, Pallas kernels for 0%

commit v1 on v0

v1 whole, which is shorter than its diff:
```python
import functools
import math

import jax
import jax.numpy as jnp
from jax import lax
from jax.experimental import pallas as pl
from jax.experimental.pallas import tpu as pltpu
from jax.sharding import PartitionSpec as P

MESH = pl.DeviceIdType.MESH
HIGHEST = lax.Precision.HIGHEST
MEMBERS = 80
BATCH = 256
HALF = 128
SLICE = 24
VAR_ROW, COS_ROW, SIN_ROW = 160, 161, 162


def dot(a, b, precision=HIGHEST):
    return jnp.dot(a, b, precision=precision, preferred_element_type=jnp.float32)


def eighth(x):
    x = x * x
    x = x * x
    return x * x


def exchange(own_ref, owner_ref, all_ref, along_y, picked, along_z, chosen, slots, sends, recvs):
    m = lax.axis_index("mem")
    c = lax.axis_index("col")
    x, core = m // 2, lax.rem(m, 2)
    z, y = c // 8, lax.rem(c, 8)
    sibling = x * 2 + 1 - core
    barrier = pltpu.get_barrier_semaphore()
    to_y = [(m, z * 8 + lax.rem(y + i, 8)) for i in range(1, 8)]
    to_z = [(m, lax.rem(z + i, 8) * 8 + y) for i in range(1, 8)]
    to_x = [(lax.rem(x + i, 4) * 2 + core, c) for i in range(1, 4)]
    for peer in to_y + to_z + to_x + [(sibling, c)]:
        pl.semaphore_signal(barrier, inc=1, device_id=peer, device_id_type=MESH)
    pl.semaphore_wait(barrier, 18)

    def copy(phase, i, src, dst, peer):
        return pltpu.make_async_remote_copy(
            src_ref=src,
            dst_ref=dst,
            send_sem=sends.at[phase, i],
            recv_sem=recvs.at[phase, i],
            device_id=peer,
            device_id_type=MESH,
        )

    def gather(phase, src, dst, mine, peers):
        for i, peer in enumerate(peers):
            copy(phase, i, src, dst.at[mine], peer).start()
        dst[mine] = src[...]
        n = len(peers) + 1
        for i, peer in enumerate(peers):
            one = copy(phase, i, src, dst.at[lax.rem(mine + n - 1 - i, n)], peer)
            one.wait_recv()
            one.wait_send()

    gather(0, own_ref, along_y, y, to_y)
    owner = owner_ref[y]
    picked[...] = along_y[lax.rem(owner, 8)]
    gather(1, picked, along_z, z, to_z)
    chosen[...] = along_z[owner // 8]
    gather(2, chosen, slots, y, to_y)
    there = (sibling, c)
    for i, peer in enumerate(to_x):
        copy(3, i, slots, all_ref.at[m], peer).start()
    copy(4, 0, slots, all_ref.at[m], there).start()
    all_ref[m] = slots[...]
    for i, peer in enumerate(to_x):
        source = lax.rem(x + 3 - i, 4) * 2 + core
        copy(3, i, slots, all_ref.at[source], peer).wait_recv()
        copy(4, i + 1, all_ref.at[source], all_ref.at[source], there).start()
    copy(4, 0, slots, all_ref.at[sibling], there).wait_recv()
    for i, peer in enumerate(to_x):
        source = lax.rem(x + 3 - i, 4) * 2
        copy(4, i + 1, all_ref.at[source + core], all_ref.at[source + 1 - core], there).wait_recv()
    for i, peer in enumerate(to_x):
        source = lax.rem(x + 3 - i, 4) * 2
        copy(3, i, slots, all_ref.at[m], peer).wait_send()
        copy(4, i + 1, all_ref.at[source + core], all_ref.at[source + core], there).wait_send()
    copy(4, 0, slots, all_ref.at[m], there).wait_send()


def lanes(x, j):
    return jnp.broadcast_to(x[:, j : j + 1], x.shape)


def pivot_rows(rows_in, columns, k, lane, board):
    for j in range(8):
        board[8 * j : 8 * j + 8, :] = columns[j]
    board[64:72, :] = rows_in
    a = {}
    for j in range(8):
        for i in range(j, 8):
            a[i, j] = jnp.broadcast_to(board[8 * j + i : 8 * j + i + 1, :], (8, HALF))
    rows = [jnp.broadcast_to(board[64 + i : 65 + i, :], (8, HALF)) for i in range(8)]
    for j in range(0, 8, 2):
        p, q, d = a[j, j], a[j + 1, j], a[j + 1, j + 1]
        r = 1.0 / (p * d - q * q)
        pi, qi, di = d * r, -(q * r), p * r
        m0 = lane == k + j
        m1 = lane == k + j + 1
        both = m0 | m1
        r0 = jnp.where(both, jnp.where(m0, 1.0, 0.0), rows[j])
        r1 = jnp.where(both, jnp.where(m1, 1.0, 0.0), rows[j + 1])
        w0 = pi * r0 + qi * r1
        w1 = qi * r0 + di * r1
        rows[j], rows[j + 1] = w0, w1
        for i in range(8):
            if i in (j, j + 1):
                continue
            if i > j:
                rows[i] = jnp.where(both, 0.0, rows[i]) - (a[i, j] * w0 + a[i, j + 1] * w1)
            else:
                rows[i] = jnp.where(both, 0.0, rows[i]) + (a[j, i] * w0 + a[j + 1, i] * w1)
        old = dict(a)
        for n in range(j + 2, 8):
            u0 = pi * old[n, j] + qi * old[n, j + 1]
            u1 = qi * old[n, j] + di * old[n, j + 1]
            for i in range(n, 8):
                a[i, n] = old[i, n] - (old[i, j] * u0 + old[i, j + 1] * u1)
            for i in range(0, j):
                a[n, i] = old[n, i] - (old[j, i] * u0 + old[j + 1, i] * u1)
            a[n, j], a[n, j + 1] = -u0, -u1
    return rows


def invert(a_ref, board):
    lane = lax.broadcasted_iota(jnp.int32, (8, HALF), 1)
    sub = lax.broadcasted_iota(jnp.int32, (8, HALF), 0)
    n = HALF // 8
    a = [a_ref[8 * v : 8 * v + 8, :] for v in range(n)]
    lower, scaled = [], []
    for block in range(n):
        k = 8 * block
        columns = {v: [lanes(a[v], k + j) for j in range(8)] for v in range(block, n)}
        rows = pivot_rows(a[block], columns[block], k, lane, board.at[pl.ds(72 * block, 72)])
        here = (lane >= k) & (lane < k + 8)
        w = rows[0]
        for i in range(1, 8):
            w = jnp.where(sub == i, rows[i], w)
        scaled.append(jnp.where(lane < k + 8, w, 0.0))
        lower.append(jnp.where(lane < k, a[block], jnp.where(lane == k + sub, 1.0, 0.0)))
        for v in range(block + 1, n):
            t = [columns[v][j] * rows[j] for j in range(8)]
            s = ((t[0] + t[1]) + (t[2] + t[3])) + ((t[4] + t[5]) + (t[6] + t[7]))
            a[v] = jnp.where(here, 0.0, a[v]) - s
    return lax.dot_general(
        jnp.concatenate(lower, 0),
        jnp.concatenate(scaled, 0),
        (((0,), (0,)), ((), ())),
        precision=HIGHEST,
        preferred_element_type=jnp.float32,
    )


def row_of(all_ref, b, row):
    return all_ref[row // SLICE, b, row % SLICE : row % SLICE + 1, :]


def rows_of(all_ref, b, first, last):
    parts = []
    while first < last:
        s, r = first // SLICE, first % SLICE
        e = min(last - first, SLICE - r)
        parts.append(all_ref[s, b, r : r + e, :])
        first += e
    return jnp.concatenate(parts, 0)


def chain(all_ref, own_ref, ownrow_ref, blockrow_ref, slab_ref, post_ref, out_ref, pool, carry, turned, cosine, sine, half, board):
    batches = pool.shape[0]

    @pl.loop(0, batches)
    def _(b):
        pool[b] = rows_of(all_ref, b, 0, MEMBERS)

    post_ref[...] = own_ref[...]
    carry[...] = jnp.where(
        lax.broadcasted_iota(jnp.int32, carry.shape, 0) == lax.broadcasted_iota(jnp.int32, carry.shape, 1), 1.0, 0.0
    )

    @pl.loop(0, batches)
    def _(b):
        priors = pool[b]
        spread = priors - jnp.sum(priors, axis=0, keepdims=True) * (1.0 / MEMBERS)
        turned[...] = spread.T * (1.0 / (MEMBERS - 1))
        gap = rows_of(all_ref, b, MEMBERS, 2 * MEMBERS) - priors
        var = row_of(all_ref, b, VAR_ROW)
        cos = row_of(all_ref, b, COS_ROW)
        sin = row_of(all_ref, b, SIN_ROW)
        cosine[...] = jnp.broadcast_to(cos, (HALF, BATCH)).T
        sine[...] = jnp.broadcast_to(sin, (HALF, BATCH)).T
        st = turned[...]
        row = lax.broadcasted_iota(jnp.int32, (BATCH, HALF), 0)
        lane = lax.broadcasted_iota(jnp.int32, (BATCH, HALF), 1)

        def weight(c, s):
            return eighth(cosine[...] * c + sine[...] * s)

        def system(t):
            part = slice(t * HALF, t * HALF + HALF)
            w = weight(cos[:, part], sin[:, part])
            return w * dot(st, spread[:, part]) + jnp.where(row == lane + t * HALF, var[:, part], 0.0)

        left, right = system(0), system(1)
        a12 = right[:HALF]
        half[0] = left[:HALF]
        first = invert(half.at[0], board.at[0])
        both = dot(jnp.concatenate([left[HALF:], gap[:, :HALF]], 0), first)
        rest = jnp.concatenate([right[HALF:], gap[:, HALF:]], 0) - dot(both, a12)
        half[1] = rest[:HALF]
        second = invert(half.at[1], board.at[1])
        x2 = dot(rest[HALF:], second)
        x1 = both[HALF:] - dot(x2, both[:HALF])
        solved = jnp.concatenate([x1, x2], 1)

        def regress(field, c, s):
            g = weight(c, s) * dot(st, field)
            return field + dot(solved, g)

        @pl.loop(b + 1, batches)
        def _(k):
            c = row_of(all_ref, k, COS_ROW)
            s = row_of(all_ref, k, SIN_ROW)
            for t in range(2):
                part = slice(t * HALF, t * HALF + HALF)
                pool[k, :, part] = regress(pool[k, :, part], c[:, part], s[:, part])

        for t in range(2):
            part = slice(t * HALF, t * HALF + HALF)
            post_ref[:, part] = regress(post_ref[:, part], ownrow_ref[0:1, part], ownrow_ref[1:2, part])
        carry[...] = regress(carry[...], blockrow_ref[0:1, :], blockrow_ref[1:2, :])

    final = carry[...][:, :MEMBERS]
    for t in range(0, slab_ref.shape[1], BATCH):
        part = slice(t, t + BATCH)
        out_ref[:, part] = dot(final, slab_ref[:, part].astype(jnp.float32)).astype(jnp.bfloat16)


def call_chain(every, own, ownrow, blockrow, slab):
    vmem = pl.BlockSpec(memory_space=pltpu.VMEM)
    batches = every.shape[1]
    return pl.pallas_call(
        chain,
        out_shape=(
            jax.ShapeDtypeStruct(own.shape, jnp.float32),
            jax.ShapeDtypeStruct(slab.shape, jnp.bfloat16),
        ),
        in_specs=[vmem] * 5,
        out_specs=(vmem, vmem),
        scratch_shapes=[
            pltpu.VMEM((batches, MEMBERS, BATCH), jnp.float32),
            pltpu.VMEM((MEMBERS, HALF), jnp.float32),
            pltpu.VMEM((BATCH, MEMBERS), jnp.float32),
            pltpu.VMEM((BATCH, HALF), jnp.float32),
            pltpu.VMEM((BATCH, HALF), jnp.float32),
            pltpu.VMEM((2, HALF, HALF), jnp.float32),
            pltpu.VMEM((2, 72 * HALF // 8, HALF), jnp.float32),
        ],
        compiler_params=pltpu.CompilerParams(vmem_limit_bytes=48 << 20),
        name="chain",
    )(every, own, ownrow, blockrow, slab)


def shards(ensemble, obs_prior, obs_value, obs_var, obs_noise, obs_block, batch_owner):
    columns_n = lax.axis_size("col")
    column = lax.axis_index("col")
    member = lax.axis_index("mem")
    blocks_own = ensemble.shape[1]
    blocks = blocks_own * columns_n
    batches = batch_owner.shape[0]
    slab = lax.all_to_all(ensemble, "mem", split_axis=1, concat_axis=0, tiled=True)[:, 0, :]
    perturbed = obs_value[None, :] + jnp.sqrt(obs_var)[None, :] * obs_noise
    angle = obs_block.astype(jnp.float32) * (math.pi / blocks)
    cos, sin = jnp.cos(angle), jnp.sin(angle)
    packed = jnp.concatenate(
        [obs_prior, perturbed, obs_var[None], cos[None], sin[None], jnp.zeros((29, BATCH), jnp.float32)], 0
    )
    mine = lax.dynamic_slice_in_dim(packed, member * SLICE, SLICE, 0)
    vmem = pl.BlockSpec(memory_space=pltpu.VMEM)
    every = pl.pallas_call(
        exchange,
        out_shape=jax.ShapeDtypeStruct((8, batches, SLICE, BATCH), jnp.float32),
        in_specs=[vmem, pl.BlockSpec(memory_space=pltpu.SMEM)],
        out_specs=vmem,
        scratch_shapes=[
            pltpu.VMEM((8, SLICE, BATCH), jnp.float32),
            pltpu.VMEM((SLICE, BATCH), jnp.float32),
            pltpu.VMEM((8, SLICE, BATCH), jnp.float32),
            pltpu.VMEM((SLICE, BATCH), jnp.float32),
            pltpu.VMEM((batches, SLICE, BATCH), jnp.float32),
            pltpu.SemaphoreType.DMA((5, 7)),
            pltpu.SemaphoreType.DMA((5, 7)),
        ],
        compiler_params=pltpu.CompilerParams(collective_id=0, has_side_effects=True, vmem_limit_bytes=32 << 20),
        name="exchange",
    )(mine, batch_owner)
    block_angle = (column * blocks_own + member).astype(jnp.float32) * (math.pi / blocks)
    blockrow = jnp.broadcast_to(jnp.stack([jnp.cos(block_angle), jnp.sin(block_angle)])[:, None], (2, HALF))
    post, done = call_chain(every, obs_prior, jnp.stack([cos, sin]), blockrow, slab)
    analysis = lax.all_to_all(done[:, None, :], "mem", split_axis=0, concat_axis=1, tiled=True)
    return (analysis, post)


def solution(mesh):
    return jax.shard_map(
        shards,
        mesh=mesh,
        in_specs=(
            P("mem", "col", None),
            P(None, "col"),
            P("col"),
            P("col"),
            P(None, "col"),
            P("col"),
            P(),
        ),
        out_specs=(P("mem", "col", None), P(None, "col")),
        check_vma=False,
    )
```

time: 2020 us -> 175 us (0.09)
  waiting for transfers between devices: 1080 us -> 0.01 us
  other arithmetic: 485 us -> 3.33 us
  blocking collectives: 227 us -> 8.27 us
  Pallas kernels: 0 us -> 145 us
  matrix products: 89.2 us -> 0 us
  local copies, waits for them, and re-layouts: 76.1 us -> 5.87 us
  between operations: 31 us -> 0.89 us
    psum x8 -> x0, waiting for transfers between devices: 1080 us -> none  [from_root(): return lax.psum(kept, axis)]
    another operation x81 -> x2, other arithmetic: 446 us -> 0.09 us  [the longest x1 0.08 us: shards(): jnp.stack([jnp.cos(block_angle), jnp.sin(block_angle)])[:, None]]
    psum x1 -> x0, blocking collectives: 227 us -> none  [from_root(): return lax.psum(kept, axis)]
    pallas_call x0 -> x2, Pallas kernels: none -> 145 us  [the longest x1 105 us: call_chain(): pl.pallas_call(chain, out_shape=(jax.ShapeDtypeStruct(own.shape, jnp.floa...]
    dot_general x152 -> x0, matrix products: 75 us -> none  [the longest x72 32.8 us: regress(): jnp.dot(solved.T, weight * covariance, precision=highest, preferred_eleme...]
    another operation x73 -> x0, local copies, waits for them, and re-layouts: 32.6 us -> none  [the longest x57 32.4 us: batch_factors(): jax.scipy.linalg.cho_solve((factor_low, True), (perturbed - priors_now).T)]
    mul x32 -> x0, other arithmetic: 22.5 us -> none  [regress(): weight * covariance]
    dynamic_update_slice x8 -> x0, local copies, waits for them, and re-layouts: 21.5 us -> none  [shards(): finished = lax.map(advance, (segments, segment_ids))]
  transfers between devices with their start and end apart: 10 -> 1, of which waited for: 8 -> 0; matrix products, arithmetic and copies ran while one was open for 1% -> 2% of each run, Pallas kernels for 0% -> 23%
where the time goes in v1:
time: 175 us; the launch traced here: 174 us
  Pallas kernels  145 us (83%)
  starting transfers between devices  10.3 us (6%)
  blocking collectives  8.27 us (5%)
  local copies, waits for them, and re-layouts  5.87 us (3%)
  other arithmetic  3.33 us (2%)
    pallas_call x1, Pallas kernels, call_chain(): pl.pallas_call(chain, out_shape=(jax.ShapeDtypeStruct(own.shape, jnp.floa...  105 us
    pallas_call x1, Pallas kernels, shards(): pl.pallas_call(exchange, out_shape=jax.ShapeDtypeStruct((8, batches, SLIC...  40.4 us
    all_to_all x1, starting transfers between devices, shards(): lax.all_to_all(ensemble, 'mem', split_axis=1, concat_axis=0, tiled=True)  10.3 us
    all_to_all x1, blocking collectives, shards(): lax.all_to_all(done[:, None, :], 'mem', split_axis=0, concat_axis=1, tile...  8.27 us
  transfers between devices with their start and end apart: 1, of which 0 were waited for; matrix products, arithmetic and copies ran while one was open for 2% of the time, Pallas kernels for 23%

profile of v1, /device:TPU:1, one launch (start us, length us, event | category | flops | bytes accessed | tf_op | source)
XLA Modules:
  0.0 174.1 jit_solution(17406386711124879181)
XLA Ops:
  0.6 0.0 copy-start.1
  0.6 1.7 copy.13
  2.4 0.0 copy-start
  2.4 10.3 %all-to-all-start = ((bf16[10,8,1024]{2,0,1:T(8,128)(2,1)}), bf16[10,8,1024]{2,0,1:T(8,128)(2,1)S(1)}, u32[]{:S(2)}, u32[]{:S(2)}) async-start(bf16[10,8,1024]{2,0,1:T(8,128)(2,1)} %copy.13), calls=%async_computation | async-start | bytes 524288 | tf_op jit(solution)/shard_map/all_to_all | solution.py:279
  12.8 0.7 sqrt.3
  13.5 0.7 fusion
  14.3 0.9 multiply_add_fusion
  15.2 1.7 %concatenate.3 = f32[192,256]{1,0:T(8,128)S(1)} concatenate(f32[80,256]{1,0:T(8,128)} %own_ref.1, f32[80,256]{1,0:T(8,128)S(1)} %multiply_add_fusion, f32[1,256]{1,0:T(1,128)} %bitcast.21, f32[1,256]{1,0:T(1,128)S(1)} %bitcast.19, f32[1,256]{1,0:T(1,128)S(1)} %bitcast.17, f32[29,256]{1,0:T(8,128)S(1)} %broadcast_in_dim.26), dimensions={0} | concatenate | bytes 393216 | tf_op jit(solution)/shard_map/concatenate | solution.py:283
  16.9 0.1 pad_maximum_fusion.1
  17.0 0.0 copy-done.1
  17.0 40.4 %exchange.1.all_ref = f32[8,8,24,256]{3,2,1,0:T(8,128)S(1)} custom-call(f32[24,256]{1,0:T(8,128)S(1)} %constant_dynamic-slice_fusion.own_ref, s32[8]{0:T(128)S(1)} %copy-done.1), custom_call_target="tpu_custom_call" | custom-call | tf_op jit(solution)/shard_map/exchange/pallas_call | solution.py:288
  57.4 0.0 all-to-all-done
  57.4 0.1 squeeze.3.slab_ref
  57.5 0.1 broadcast_in_dim.27.blockrow_ref
  57.6 0.0 copy-done
  57.6 105.1 %chain.1 = (f32[80,256]{1,0:T(8,128)}, bf16[80,1024]{1,0:T(8,128)(2,1)S(1)}) custom-call(f32[8,8,24,256]{3,2,1,0:T(8,128)S(1)} %exchange.1.all_ref, f32[80,256]{1,0:T(8,128)S(1)} %copy-done, f32[2,256]{1,0:T(2,128)S(1)} %pad_maximum_fusion.ownrow_ref, f32[2,128]{1,0:T(2,128)S(1)} %broadcast_in_dim.27.blockrow_ref, bf16[80,1024]{1,0:T(8,128)(2,1)S(1)} %squeeze.3.slab_ref), custom_call_target="tpu_custom_call" | custom-call | tf_op jit(solution)/shard_map/chain/pallas_call | solution.py:250
  162.7 0.5 broadcast.4
  163.2 0.7 reduce.1
  163.9 0.1 reshape.9
  164.0 8.3 %all_to_all.33 = bf16[8,2,5120]{2,1,0:T(2,128)(2,1)S(1)} all-to-all(bf16[8,2,5120]{2,1,0:T(2,128)(2,1)S(1)} %reshape.9), channel_id=1, replica_groups=mesh['mem'=8,'col'=64] {'mem'}, dimensions={0} | all-to-all | bytes 327680 | tf_op jit(solution)/shard_map/all_to_all | solution.py:308
  172.2 0.1 reshape.10
  172.4 0.9 reduce
  173.3 0.1 all_to_all.28
  173.4 0.8 copy.15
  (3 shorter events, 0.0 us)
Async XLA Ops:
  0.6 16.4 %copy-start.1 = (s32[8]{0:T(128)S(1)}, s32[8]{0:T(128)}, u32[]{:S(2)}) copy-start(s32[8]{0:T(128)} %owner_ref.1) | copy-start | bytes 100
  2.4 55.2 %copy-start = (f32[80,256]{1,0:T(8,128)S(1)}, f32[80,256]{1,0:T(8,128)}, u32[]{:S(2)}) copy-start(f32[80,256]{1,0:T(8,128)} %own_ref.1) | copy-start | bytes 245764
  2.4 55.1 %all-to-all-start = ((bf16[10,8,1024]{2,0,1:T(8,128)(2,1)}), bf16[10,8,1024]{2,0,1:T(8,128)(2,1)S(1)}, u32[]{:S(2)}, u32[]{:S(2)}) async-start(bf16[10,8,1024]{2,0,1:T(8,128)(2,1)} %copy.13), calls=%async_computation | async-start | bytes 524288 | tf_op jit(solution)/shard_map/all_to_all | solution.py:279

commit v2 on v1

v2 whole, which is shorter than its diff:
```python
import functools
import math

import jax
import jax.numpy as jnp
from jax import lax
from jax.experimental import pallas as pl
from jax.experimental.pallas import tpu as pltpu
from jax.sharding import PartitionSpec as P

MESH = pl.DeviceIdType.MESH
HIGHEST = lax.Precision.HIGHEST
MEMBERS = 80
BATCH = 256
HALF = 128
GROUPS = 6
TILES = 8 * GROUPS


def dot(a, b, precision=HIGHEST):
    return jnp.dot(a, b, precision=precision, preferred_element_type=jnp.float32)


def eighth(x):
    x = x * x
    x = x * x
    return x * x


def lanes(x, j):
    return jnp.broadcast_to(x[:, j : j + 1], x.shape)


def pivot_rows(rows_in, columns, k, lane, board):
    for j in range(8):
        board[8 * j : 8 * j + 8, :] = columns[j]
    board[64:72, :] = rows_in
    a = {}
    for j in range(8):
        for i in range(j, 8):
            a[i, j] = jnp.broadcast_to(board[8 * j + i : 8 * j + i + 1, :], (8, HALF))
    rows = [jnp.broadcast_to(board[64 + i : 65 + i, :], (8, HALF)) for i in range(8)]
    for j in range(0, 8, 2):
        p, q, d = a[j, j], a[j + 1, j], a[j + 1, j + 1]
        r = 1.0 / (p * d - q * q)
        pi, qi, di = d * r, -(q * r), p * r
        m0 = lane == k + j
        m1 = lane == k + j + 1
        both = m0 | m1
        r0 = jnp.where(both, jnp.where(m0, 1.0, 0.0), rows[j])
        r1 = jnp.where(both, jnp.where(m1, 1.0, 0.0), rows[j + 1])
        w0 = pi * r0 + qi * r1
        w1 = qi * r0 + di * r1
        rows[j], rows[j + 1] = w0, w1
        for i in range(8):
            if i in (j, j + 1):
                continue
            if i > j:
                rows[i] = jnp.where(both, 0.0, rows[i]) - (a[i, j] * w0 + a[i, j + 1] * w1)
            else:
                rows[i] = jnp.where(both, 0.0, rows[i]) + (a[j, i] * w0 + a[j + 1, i] * w1)
        old = dict(a)
        for n in range(j + 2, 8):
            u0 = pi * old[n, j] + qi * old[n, j + 1]
            u1 = qi * old[n, j] + di * old[n, j + 1]
            for i in range(n, 8):
                a[i, n] = old[i, n] - (old[i, j] * u0 + old[i, j + 1] * u1)
            for i in range(0, j):
                a[n, i] = old[n, i] - (old[j, i] * u0 + old[j + 1, i] * u1)
            a[n, j], a[n, j + 1] = -u0, -u1
    return rows


def invert(a_ref, board):
    lane = lax.broadcasted_iota(jnp.int32, (8, HALF), 1)
    sub = lax.broadcasted_iota(jnp.int32, (8, HALF), 0)
    n = HALF // 8
    a = [a_ref[8 * v : 8 * v + 8, :] for v in range(n)]
    lower, scaled = [], []
    for block in range(n):
        k = 8 * block
        columns = {v: [lanes(a[v], k + j) for j in range(8)] for v in range(block, n)}
        rows = pivot_rows(a[block], columns[block], k, lane, board.at[pl.ds(72 * block, 72)])
        here = (lane >= k) & (lane < k + 8)
        w = rows[0]
        for i in range(1, 8):
            w = jnp.where(sub == i, rows[i], w)
        scaled.append(jnp.where(lane < k + 8, w, 0.0))
        lower.append(jnp.where(lane < k, a[block], jnp.where(lane == k + sub, 1.0, 0.0)))
        for v in range(block + 1, n):
            t = [columns[v][j] * rows[j] for j in range(8)]
            s = ((t[0] + t[1]) + (t[2] + t[3])) + ((t[4] + t[5]) + (t[6] + t[7]))
            a[v] = jnp.where(here, 0.0, a[v]) - s
    return lax.dot_general(
        jnp.concatenate(lower, 0),
        jnp.concatenate(scaled, 0),
        (((0,), (0,)), ((), ())),
        precision=HIGHEST,
        preferred_element_type=jnp.float32,
    )


def regress_all(
    ens_ref, prior_ref, value_ref, var_ref, noise_ref, angle_ref, block_ref, owner_ref,
    out_ref, post_ref,
    tiles, along_y, picked, along_z, along_z_rest, chosen, every, every_rest, wide, going, coming, back,
    state, pool, target, facts, carry, turned, cosine, sine, half, board, sends, recvs,
):
    m = lax.axis_index("mem")
    c = lax.axis_index("col")
    x, core = m // 2, lax.rem(m, 2)
    z, y = c // 8, lax.rem(c, 8)
    batches = pool.shape[0]
    rows = ens_ref.shape[0]
    to_y = [(m, z * 8 + lax.rem(y + i, 8)) for i in range(1, 8)]
    to_z = [(m, lax.rem(z + i, 8) * 8 + y) for i in range(1, 8)]
    to_m = [(lax.rem(m + i, 8), c) for i in range(1, 8)]
    to_x = [(lax.rem(x + i, 4) * 2 + core, c) for i in range(1, 4)]
    there = (x * 2 + 1 - core, c)
    barrier = pltpu.get_barrier_semaphore()
    for peer in to_y + to_z + to_m:
        pl.semaphore_signal(barrier, inc=1, device_id=peer, device_id_type=MESH)

    cos, sin = jnp.cos(angle_ref[...]), jnp.sin(angle_ref[...])
    perturbed = value_ref[...] + jnp.sqrt(var_ref[...]) * noise_ref[...]
    for g in range(10):
        for t in range(2):
            lane = slice(t * HALF, t * HALF + HALF)
            tiles[2 * g + t] = prior_ref[8 * g : 8 * g + 8, lane]
            tiles[20 + 2 * g + t] = perturbed[8 * g : 8 * g + 8, lane]
    for t in range(2):
        lane = slice(t * HALF, t * HALF + HALF)
        tiles[40 + t] = jnp.concatenate(
            [var_ref[:, lane], cos[:, lane], sin[:, lane], jnp.zeros((5, HALF), jnp.float32)], 0
        )
    for t in range(42, TILES):
        tiles[t] = jnp.zeros((8, HALF), jnp.float32)
    pl.semaphore_wait(barrier, 21)

    def copy(phase, i, src, dst, peer):
        return pltpu.make_async_remote_copy(
            src_ref=src,
            dst_ref=dst,
            send_sem=sends.at[phase, i],
            recv_sem=recvs.at[phase, i],
            device_id=peer,
            device_id_type=MESH,
        )

    piece = lambda k: tiles.at[m * GROUPS + jnp.minimum(k, GROUPS - 1)]
    for i, peer in enumerate(to_y):
        copy(0, i, piece(lax.rem(y + i + 1, 8)), along_y.at[y], peer).start()
    along_y[y] = tiles[m * GROUPS + jnp.minimum(y, GROUPS - 1)]

    wide[...] = ens_ref[...].astype(jnp.float32)
    for g in range(8):
        going[g] = wide[:, g, :].astype(jnp.bfloat16)

    def wait_recv(phase, i, src, dst, peer):
        copy(phase, i, src, dst, peer).wait_recv()

    for i, peer in enumerate(to_y):
        wait_recv(0, i, tiles.at[0], along_y.at[lax.rem(y + 7 - i, 8)], peer)
    owners = [owner_ref[j] for j in range(batches)]
    for j in range(batches):
        picked[j] = along_y[lax.rem(owners[j], 8)]
    rest = pl.ds(1, batches - 1)
    for i, peer in enumerate(to_z):
        copy(1, i, picked.at[0], along_z.at[z], peer).start()
    for i, peer in enumerate(to_z):
        copy(2, i, picked.at[rest], along_z_rest.at[z], peer).start()
    along_z[z] = picked[0]
    along_z_rest[z] = picked[1:]
    for i, peer in enumerate(to_z):
        wait_recv(1, i, picked.at[0], along_z.at[lax.rem(z + 7 - i, 8)], peer)
    chosen[0] = along_z[owners[0] // 8]
    for i, peer in enumerate(to_y):
        copy(3, i, chosen.at[0], every.at[m, y], peer).start()
    every[m, y] = chosen[0]
    for i, peer in enumerate(to_y):
        wait_recv(3, i, chosen.at[0], every.at[m, lax.rem(y + 7 - i, 8)], peer)
    used = pl.ds(0, GROUPS)
    mine = every.at[m, used]
    for i, peer in enumerate(to_x):
        copy(4, i, mine, mine, peer).start()
    copy(5, 0, mine, mine, there).start()

    for i, peer in enumerate(to_z):
        wait_recv(2, i, picked.at[rest], along_z_rest.at[lax.rem(z + 7 - i, 8)], peer)
    for j in range(1, batches):
        chosen[j] = along_z_rest[owners[j] // 8, j - 1]
    for i, peer in enumerate(to_y):
        copy(6, i, chosen.at[rest], every_rest.at[m, y], peer).start()
    every_rest[m, y] = chosen[1:]

    def source(i):
        return lax.rem(x + 3 - i, 4) * 2

    for i, peer in enumerate(to_x):
        got = every.at[source(i) + core, used]
        wait_recv(4, i, got, got, peer)
        copy(5, i + 1, got, got, there).start()
    for i, peer in enumerate(to_m):
        copy(9, i, going.at[lax.rem(m + i + 1, 8)], coming.at[m], peer).start()
    coming[m] = going[m]
    wait_recv(5, 0, mine, every.at[there[0], used], there)
    for i, peer in enumerate(to_x):
        got = every.at[source(i) + 1 - core, used]
        wait_recv(5, i + 1, got, got, there)

    def unpack(get, b):
        for t in range(40):
            g, lane = t % 20 // 2, slice(t % 2 * HALF, t % 2 * HALF + HALF)
            to = pool if t < 20 else target
            to[b, 8 * g : 8 * g + 8, lane] = get(t // GROUPS, t % GROUPS)
        for t in range(40, 42):
            lane = slice(t % 2 * HALF, t % 2 * HALF + HALF)
            facts[b, :, lane] = get(t // GROUPS, t % GROUPS)

    unpack(lambda p, q: every[p, q], 0)
    post_ref[...] = prior_ref[...]
    carry[...] = jnp.where(
        lax.broadcasted_iota(jnp.int32, carry.shape, 0) == lax.broadcasted_iota(jnp.int32, carry.shape, 1), 1.0, 0.0
    )

    @pl.loop(0, batches)
    def _(b):
        priors = pool[b]
        spread = priors - jnp.sum(priors, axis=0, keepdims=True) * (1.0 / MEMBERS)
        turned[...] = spread.T * (1.0 / (MEMBERS - 1))
        gap = target[b] - priors
        fact = facts[b]
        var, cos, sin = fact[0:1], fact[1:2], fact[2:3]
        cosine[...] = jnp.broadcast_to(cos, (HALF, BATCH)).T
        sine[...] = jnp.broadcast_to(sin, (HALF, BATCH)).T
        st = turned[...]
        row = lax.broadcasted_iota(jnp.int32, (BATCH, HALF), 0)
        lane = lax.broadcasted_iota(jnp.int32, (BATCH, HALF), 1)

        def weight(c, s):
            return eighth(cosine[...] * c + sine[...] * s)

        def system(t):
            part = slice(t * HALF, t * HALF + HALF)
            w = weight(cos[:, part], sin[:, part])
            return w * dot(st, spread[:, part]) + jnp.where(row == lane + t * HALF, var[:, part], 0.0)

        left, right = system(0), system(1)
        a12 = right[:HALF]
        half[0] = left[:HALF]

        @pl.when(b == 0)
        def _():
            for i, peer in enumerate(to_y):
                wait_recv(6, i, chosen.at[rest], every_rest.at[m, lax.rem(y + 7 - i, 8)], peer)
            part = every_rest.at[m, used]
            for i, peer in enumerate(to_x):
                copy(7, i, part, part, peer).start()
            copy(8, 0, part, part, there).start()

        first = invert(half.at[0], board.at[0])
        both = dot(jnp.concatenate([left[HALF:], gap[:, :HALF]], 0), first)
        schur = jnp.concatenate([right[HALF:], gap[:, HALF:]], 0) - dot(both, a12)
        half[1] = schur[:HALF]
        second = invert(half.at[1], board.at[1])

        @pl.when(b == 0)
        def _():
            for i, peer in enumerate(to_x):
                got = every_rest.at[source(i) + core, used]
                wait_recv(7, i, got, got, peer)
                copy(8, i + 1, got, got, there).start()

        x2 = dot(schur[HALF:], second)
        x1 = both[HALF:] - dot(x2, both[:HALF])
        solved = jnp.concatenate([x1, x2], 1)

        def regress(field, c, s):
            g = weight(c, s) * dot(st, field)
            return field + dot(solved, g)

        for t in range(2):
            part = slice(t * HALF, t * HALF + HALF)
            c, s = tiles[40 + t][1:2], tiles[40 + t][2:3]
            post_ref[:, part] = regress(post_ref[:, part], c, s)
        carry[...] = regress(carry[...], block_ref[0:1, :], block_ref[1:2, :])

        @pl.when(b == 0)
        def _():
            wait_recv(8, 0, every_rest.at[m, used], every_rest.at[there[0], used], there)
            for i, peer in enumerate(to_x):
                got = every_rest.at[source(i) + 1 - core, used]
                wait_recv(8, i + 1, got, got, there)

            @pl.loop(1, batches)
            def _(k):
                unpack(lambda p, q: every_rest[p, q, k - 1], k)

            for i, peer in enumerate(to_m):
                wait_recv(9, i, going.at[0], coming.at[lax.rem(m + 7 - i, 8)], peer)
            for g in range(8):
                state[rows * g : rows * g + rows, :] = coming[g].astype(jnp.float32)

        @pl.loop(b + 1, batches)
        def _(k):
            c = facts[k][1:2]
            s = facts[k][2:3]
            for t in range(2):
                part = slice(t * HALF, t * HALF + HALF)
                pool[k, :, part] = regress(pool[k, :, part], c[:, part], s[:, part])

    for i, peer in enumerate(to_y):
        copy(0, i, tiles.at[0], along_y.at[y], peer).wait_send()
        copy(3, i, chosen.at[0], every.at[m, y], peer).wait_send()
        copy(6, i, chosen.at[rest], every_rest.at[m, y], peer).wait_send()
    for i, peer in enumerate(to_z):
        copy(1, i, picked.at[0], along_z.at[z], peer).wait_send()
        copy(2, i, picked.at[rest], along_z_rest.at[z], peer).wait_send()
    part = every_rest.at[m, used]
    for i, peer in enumerate(to_x):
        copy(4, i, mine, mine, peer).wait_send()
        copy(7, i, part, part, peer).wait_send()
    for i in range(4):
        copy(5, i, mine, mine, there).wait_send()
        copy(8, i, part, part, there).wait_send()
    for i, peer in enumerate(to_m):
        copy(9, i, going.at[0], coming.at[m], peer).wait_send()

    final = carry[...][:, :MEMBERS]
    for t in range(0, state.shape[1], BATCH):
        part = slice(t, t + BATCH)
        state[:, part] = dot(final, state[:, part])
    for g in range(8):
        going[g] = state[rows * g : rows * g + rows, :].astype(jnp.bfloat16)
    for i, peer in enumerate(to_m):
        copy(10, i, going.at[lax.rem(m + i + 1, 8)], back.at[m], peer).start()
    back[m] = going[m]
    for i, peer in enumerate(to_m):
        one = copy(10, i, going.at[0], back.at[lax.rem(m + 7 - i, 8)], peer)
        one.wait_recv()
        one.wait_send()
    for g in range(8):
        wide[:, g, :] = back[g].astype(jnp.float32)
    out_ref[...] = wide[...].astype(jnp.bfloat16)


def shards(ensemble, obs_prior, obs_value, obs_var, obs_noise, obs_block, batch_owner):
    columns_n = lax.axis_size("col")
    column = lax.axis_index("col")
    member = lax.axis_index("mem")
    rows, blocks_own, cells = ensemble.shape
    blocks = blocks_own * columns_n
    batches = batch_owner.shape[0]
    angle = obs_block.astype(jnp.float32) * (math.pi / blocks)
    block_angle = (column * blocks_own + member).astype(jnp.float32) * (math.pi / blocks)
    blockrow = jnp.broadcast_to(jnp.stack([jnp.cos(block_angle), jnp.sin(block_angle)])[:, None], (2, HALF))
    vmem = pl.BlockSpec(memory_space=pltpu.VMEM)
    f32, bf16 = jnp.float32, jnp.bfloat16
    return pl.pallas_call(
        regress_all,
        out_shape=(
            jax.ShapeDtypeStruct(ensemble.shape, bf16),
            jax.ShapeDtypeStruct(obs_prior.shape, f32),
        ),
        in_specs=[vmem] * 7 + [pl.BlockSpec(memory_space=pltpu.SMEM)],
        out_specs=(vmem, vmem),
        scratch_shapes=[
            pltpu.VMEM((TILES, 8, HALF), f32),
            pltpu.VMEM((8, 8, HALF), f32),
            pltpu.VMEM((batches, 8, HALF), f32),
            pltpu.VMEM((8, 8, HALF), f32),
            pltpu.VMEM((8, batches - 1, 8, HALF), f32),
            pltpu.VMEM((batches, 8, HALF), f32),
            pltpu.VMEM((8, 8, 8, HALF), f32),
            pltpu.VMEM((8, 8, batches - 1, 8, HALF), f32),
            pltpu.VMEM(ensemble.shape, f32),
            pltpu.VMEM((8, rows, cells), bf16),
            pltpu.VMEM((8, rows, cells), bf16),
            pltpu.VMEM((8, rows, cells), bf16),
            pltpu.VMEM((MEMBERS, cells), f32),
            pltpu.VMEM((batches, MEMBERS, BATCH), f32),
            pltpu.VMEM((batches, MEMBERS, BATCH), f32),
            pltpu.VMEM((batches, 8, BATCH), f32),
            pltpu.VMEM((MEMBERS, HALF), f32),
            pltpu.VMEM((BATCH, MEMBERS), f32),
            pltpu.VMEM((BATCH, HALF), f32),
            pltpu.VMEM((BATCH, HALF), f32),
            pltpu.VMEM((2, HALF, HALF), f32),
            pltpu.VMEM((2, 72 * HALF // 8, HALF), f32),
            pltpu.SemaphoreType.DMA((11, 7)),
            pltpu.SemaphoreType.DMA((11, 7)),
        ],
        compiler_params=pltpu.CompilerParams(collective_id=0, has_side_effects=True, vmem_limit_bytes=48 << 20),
        name="regress_all",
    )(
        ensemble, obs_prior, obs_value[None], obs_var[None], obs_noise, angle[None], blockrow, batch_owner
    )


def solution(mesh):
    return jax.shard_map(
        shards,
        mesh=mesh,
        in_specs=(
            P("mem", "col", None),
            P(None, "col"),
            P("col"),
            P("col"),
            P(None, "col"),
            P("col"),
            P(),
        ),
        out_specs=(P("mem", "col", None), P(None, "col")),
        check_vma=False,
    )
```

time: 175 us -> 160 us (0.914)
  starting transfers between devices: 10.3 us -> 0 us
  Pallas kernels: 145 us -> 154 us
  blocking collectives: 8.27 us -> 0 us
  other arithmetic: 3.33 us -> 0.08 us
    all_to_all x1 -> x0, starting transfers between devices: 10.3 us -> none  [shards(): lax.all_to_all(ensemble, 'mem', split_axis=1, concat_axis=0, tiled=True)]
    all_to_all x1 -> x0, blocking collectives: 8.27 us -> none  [shards(): lax.all_to_all(done[:, None, :], 'mem', split_axis=0, concat_axis=1, tile...]
    pallas_call x2 -> x1, Pallas kernels: 145 us -> 154 us  [shards(): pl.pallas_call(regress_all, out_shape=(jax.ShapeDtypeStruct(ensemble.shap...]
    unnamed x8 -> x16, local copies, waits for them, and re-layouts: 2.72 us -> 5.29 us
  transfers between devices with their start and end apart: 1 -> 0, of which waited for: 0 -> 0; matrix products, arithmetic and copies ran while one was open for 2% -> 0% of each run, Pallas kernels for 23% -> 0%
where the time goes in v2:
time: 160 us
  Pallas kernels  154 us (96%)
  local copies, waits for them, and re-layouts  5.36 us (3%)
    pallas_call x1, Pallas kernels, shards(): pl.pallas_call(regress_all, out_shape=(jax.ShapeDtypeStruct(ensemble.shap...  154 us
    unnamed x16, local copies, waits for them, and re-layouts  5.29 us

profile of v2, /device:TPU:1, one launch (start us, length us, event | category | flops | bytes accessed | tf_op | source)
XLA Modules:
  0.0 159.8 jit_solution(1947297479860624186)
XLA Ops:
  0.8 0.1 pad_maximum_fusion
  0.9 0.0 copy-start.6
  0.9 0.1 broadcast_in_dim.18.block_ref
  0.9 0.6 copy-done.6
  1.5 0.0 copy-start.4
  1.6 0.0 copy-start.3
  1.6 0.0 copy-start.5
  1.6 0.7 copy-done.4
  2.2 0.0 copy-done.3
  2.2 0.0 copy-done.5
  2.2 0.0 copy-start
  2.2 0.9 copy-done
  3.2 0.0 copy-start.1
  3.2 0.9 copy-done.1
  4.0 0.0 copy-start.2
  4.0 0.9 copy-done.2
  4.9 153.5 %regress_all.1 = (bf16[10,8,1024]{2,1,0:T(8,128)(2,1)S(1)}, f32[80,256]{1,0:T(8,128)S(1)}) custom-call(bf16[10,8,1024]{2,1,0:T(8,128)(2,1)S(1)} %copy-done, f32[80,256]{1,0:T(8,128)S(1)} %copy-done.1, f32[1,256]{1,0:T(1,128)S(1)} %bitcast.6, f32[1,256]{1,0:T(1,128)S(1)} %bitcast.7, f32[80,256]{1,0:T(8,128)S(1)} %copy-done.2, f32[1,256]{1,0:T(1,128)S(1)} %bitcast.5, ...), custom_call_target="tpu_custom_call" | custom-call | tf_op jit(solution)/shard_map/regress_all/pallas_call | solution.py:359
  158.5 0.7 copy.11
  159.1 0.6 copy.12
  (1 shorter events, 0.0 us)
Async XLA Ops:
  0.9 0.7 copy-start.6
  1.5 0.7 copy-start.4
  1.6 0.7 copy-start.3
  1.6 0.7 copy-start.5
  2.2 0.9 copy-start
  3.2 0.9 copy-start.1
  4.0 0.9 copy-start.2

commit v3 on v2

--- a/solution.py
+++ b/solution.py
@@ -9,7 +9,6 @@
 from jax.sharding import PartitionSpec as P
 
 MESH = pl.DeviceIdType.MESH
-HIGHEST = lax.Precision.HIGHEST
 MEMBERS = 80
 BATCH = 256
 HALF = 128
@@ -17,8 +16,38 @@
 TILES = 8 * GROUPS
 
 
-def dot(a, b, precision=HIGHEST):
-    return jnp.dot(a, b, precision=precision, preferred_element_type=jnp.float32)
+def split(x, n):
+    parts = []
+    for _ in range(n - 1):
+        parts.append(x.astype(jnp.bfloat16))
+        x = x - parts[-1].astype(jnp.float32)
+    parts.append(x.astype(jnp.bfloat16))
+    return parts
+
+
+def once(a, b):
+    return jnp.dot(a, b, preferred_element_type=jnp.float32)
+
+
+def cat0(*v):
+    return jnp.concatenate(v, 0)
+
+
+def cat1(*v):
+    return jnp.concatenate(v, 1)
+
+
+def narrow(a, b):
+    p, q = split(a, 3), split(b, 3)
+    front = cat1(p[0], p[1])
+    return (once(cat1(p[0], p[2]), cat0(q[2], q[0])) + once(front, cat0(q[1], q[1]))) + once(front, cat0(q[0], q[0]))
+
+
+def wide_sum(stack, n, q):
+    top = once(stack, q[0])
+    middle = once(stack[: 2 * n], q[1])
+    low = once(stack[:n], q[2])
+    return top[:n] + ((top[n : 2 * n] + middle[:n]) + (top[2 * n :] + middle[n:] + low))
 
 
 def eighth(x):
@@ -70,8 +99,7 @@
             a[n, j], a[n, j + 1] = -u0, -u1
     return rows
 
-
-def invert(a_ref, board):
+def invert(a_ref, board, between):
     lane = lax.broadcasted_iota(jnp.int32, (8, HALF), 1)
     sub = lax.broadcasted_iota(jnp.int32, (8, HALF), 0)
     n = HALF // 8
@@ -91,27 +119,156 @@
             t = [columns[v][j] * rows[j] for j in range(8)]
             s = ((t[0] + t[1]) + (t[2] + t[3])) + ((t[4] + t[5]) + (t[6] + t[7]))
             a[v] = jnp.where(here, 0.0, a[v]) - s
-    return lax.dot_general(
-        jnp.concatenate(lower, 0),
-        jnp.concatenate(scaled, 0),
-        (((0,), (0,)), ((), ())),
-        precision=HIGHEST,
-        preferred_element_type=jnp.float32,
-    )
+        between()
+    return narrow(jnp.concatenate(lower, 0).T, jnp.concatenate(scaled, 0))
+
+
+class Regression:
+    def __init__(self, p, turned, turned_low, cosine, sine, solved, gains):
+        self.p = p
+        self.turned, self.turned_low, self.cosine, self.sine = turned, turned_low, cosine, sine
+        self.solved, self.gains = solved, gains
+
+    def weight(self, c, s):
+        return eighth(self.cosine[self.p] * c + self.sine[self.p] * s)
+
+    def across(self, field):
+        f = split(field, 3)
+        total = once(self.turned_low[self.p], cat0(f[1], f[0], f[2])) + once(self.turned[self.p], cat0(f[0], f[0], f[1]))
+        return total * (1.0 / (MEMBERS - 1))
+
+    def gain(self, i, field, c, s):
+        for q, part in enumerate(split(self.weight(c, s) * self.across(field), 3)):
+            self.gains[i, q] = part
+
+    def add(self, i, field):
+        return field + wide_sum(self.solved[self.p], MEMBERS, [self.gains[i, q] for q in range(3)])
+
+
+def later(regression, fields):
+    for i, (read, write, c, s) in enumerate(fields):
+        regression.gain(i % 2, read(), c(), s())
+        yield
+        write(regression.add(i % 2, read()))
+        yield
+
+
+def columns_of(ref, k, facts):
+    for t in range(2):
+        part = slice(t * HALF, t * HALF + HALF)
+
+        def write(value, part=part):
+            ref[k, :, part] = value
+
+        yield (
+            lambda part=part: ref[k, :, part],
+            write,
+            lambda part=part: facts[k, 1:2, part],
+            lambda part=part: facts[k, 2:3, part],
+        )
+
+
+def assimilate(batches, pool, target, facts, carry, blockrow, turned, turned_low, cosine, sine, solved, gains, half, board, hooks):
+    own = pool.shape[0] - 1
+    turned[1] = jnp.zeros(turned.shape[1:], turned.dtype)
+    turned_low[1] = jnp.zeros(turned.shape[1:], turned.dtype)
+    cosine[1] = jnp.zeros(cosine.shape[1:], jnp.float32)
+    sine[1] = jnp.zeros(cosine.shape[1:], jnp.float32)
+    solved[1] = jnp.zeros(solved.shape[1:], solved.dtype)
+    row = lax.broadcasted_iota(jnp.int32, carry.shape, 0)
+    carry[...] = jnp.where(row == lax.broadcasted_iota(jnp.int32, carry.shape, 1), 1.0, 0.0)
+
+    def keep(value):
+        carry[...] = value
+
+    mine = list(columns_of(pool, own, facts)) + [
+        (lambda: carry[...], keep, lambda: blockrow[0:1, :], lambda: blockrow[1:2, :])
+    ]
+    factors = (turned, turned_low, cosine, sine, solved, gains)
+
+    @pl.loop(0, batches)
+    def _(b):
+        now = lax.rem(b, 2)
+        here = Regression(now, *factors)
+        before = Regression(1 - now, *factors)
+        priors = pool[b]
+        spread = priors - jnp.sum(priors, axis=0, keepdims=True) * (1.0 / MEMBERS)
+        s0, s1, s2 = split(spread, 3)
+        turned[now] = cat0(s0, s1, s0).T
+        turned_low[now] = cat0(s1, s2, s0).T
+        gap = target[b] - priors
+        fact = facts[b]
+        var, cos, sin = fact[0:1], fact[1:2], fact[2:3]
+        cosine[now] = jnp.broadcast_to(cos, (HALF, BATCH)).T
+        sine[now] = jnp.broadcast_to(sin, (HALF, BATCH)).T
+        row = lax.broadcasted_iota(jnp.int32, (BATCH, HALF), 0)
+        lane = lax.broadcasted_iota(jnp.int32, (BATCH, HALF), 1)
+        covariance = here.across(spread)
+
+        def system(t):
+            part = slice(t * HALF, t * HALF + HALF)
+            w = here.weight(cos[:, part], sin[:, part])
+            return w * covariance[:, part] + jnp.where(row == lane + t * HALF, var[:, part], 0.0)
+
+        left, right = system(0), system(1)
+        a12 = right[:HALF]
+        half[0] = left[:HALF]
+        hooks[0](b)
+        fields = list(mine)
+        for i in range(batches - 2):
+            fields += columns_of(pool, b + 2 - 1 + i, facts)
+        steps = later(before, fields)
+        done = object()
+        between = lambda: next(steps, done)
+        first = invert(half.at[0], board.at[0], between)
+        both = narrow(cat0(left[HALF:], gap[:, :HALF]), first)
+        schur = cat0(right[HALF:], gap[:, HALF:]) - narrow(both, a12)
+        half[1] = schur[:HALF]
+        second = invert(half.at[1], board.at[1], between)
+        for _ in steps:
+            pass
+        hooks[1](b)
+        x2 = narrow(schur[HALF:], second)
+        x1 = both[HALF:] - narrow(x2, both[:HALF])
+        solved[now] = cat0(*split(cat1(x1, x2), 3))
+        hooks[2](b)
+        for _ in later(here, columns_of(pool, b + 1, facts)):
+            pass
+
+    return Regression((batches - 1) % 2, *factors), mine
 
 
 def regress_all(
-    ens_ref, prior_ref, value_ref, var_ref, noise_ref, angle_ref, block_ref, owner_ref,
+    ens_hbm, prior_hbm, value_hbm, var_hbm, noise_hbm, place_hbm, owner_ref,
     out_ref, post_ref,
+    ens, prior, value, var_in, noise, place, blockrow,
     tiles, along_y, picked, along_z, along_z_rest, chosen, every, every_rest, wide, going, coming, back,
-    state, pool, target, facts, carry, turned, cosine, sine, half, board, sends, recvs,
+    state, pool, target, facts, carry, turned, turned_low, cosine, sine, solved, gains, half, board,
+    loads, sends, recvs,
 ):
     m = lax.axis_index("mem")
     c = lax.axis_index("col")
     x, core = m // 2, lax.rem(m, 2)
     z, y = c // 8, lax.rem(c, 8)
-    batches = pool.shape[0]
-    rows = ens_ref.shape[0]
+    batches = target.shape[0]
+    own = pool.shape[0] - 1
+    rows, blocks_own, _ = ens.shape
+    step = math.pi / (blocks_own * lax.axis_size("col"))
+    arrived = [
+        pltpu.make_async_copy(far, near, loads.at[i])
+        for i, (far, near) in enumerate(
+            [
+                (value_hbm, value),
+                (var_hbm, var_in),
+                (place_hbm, place),
+                (prior_hbm, prior),
+                (noise_hbm, noise),
+                (ens_hbm, ens),
+            ]
+        )
+    ]
+    for load in arrived:
+        load.start()
     to_y = [(m, z * 8 + lax.rem(y + i, 8)) for i in range(1, 8)]
     to_z = [(m, lax.rem(z + i, 8) * 8 + y) for i in range(1, 8)]
     to_m = [(lax.rem(m + i, 8), c) for i in range(1, 8)]
@@ -121,20 +278,23 @@
     for peer in to_y + to_z + to_m:
         pl.semaphore_signal(barrier, inc=1, device_id=peer, device_id_type=MESH)
 
-    cos, sin = jnp.cos(angle_ref[...]), jnp.sin(angle_ref[...])
-    perturbed = value_ref[...] + jnp.sqrt(var_ref[...]) * noise_ref[...]
+    here = jnp.full((8, HALF), (c * blocks_own + m).astype(jnp.float32) * step)
+    blockrow[...] = jnp.where(lax.broadcasted_iota(jnp.int32, (8, HALF), 0) == 0, jnp.cos(here), jnp.sin(here))
+    for t in range(42, TILES):
+        tiles[t] = jnp.zeros((8, HALF), jnp.float32)
+    for load in arrived[:5]:
+        load.wait()
+    angle = place[...].astype(jnp.float32) * step
+    cos, sin = jnp.cos(angle), jnp.sin(angle)
+    perturbed = value[...] + jnp.sqrt(var_in[...]) * noise[...]
     for g in range(10):
         for t in range(2):
             lane = slice(t * HALF, t * HALF + HALF)
-            tiles[2 * g + t] = prior_ref[8 * g : 8 * g + 8, lane]
+            tiles[2 * g + t] = prior[8 * g : 8 * g + 8, lane]
             tiles[20 + 2 * g + t] = perturbed[8 * g : 8 * g + 8, lane]
+    fact = jnp.concatenate([var_in[...], cos, sin, jnp.zeros((5, BATCH), jnp.float32)], 0)
     for t in range(2):
-        lane = slice(t * HALF, t * HALF + HALF)
-        tiles[40 + t] = jnp.concatenate(
-            [var_ref[:, lane], cos[:, lane], sin[:, lane], jnp.zeros((5, HALF), jnp.float32)], 0
-        )
-    for t in range(42, TILES):
-        tiles[t] = jnp.zeros((8, HALF), jnp.float32)
+        tiles[40 + t] = fact[:, t * HALF : t * HALF + HALF]
     pl.semaphore_wait(barrier, 21)
 
     def copy(phase, i, src, dst, peer):
@@ -152,9 +312,16 @@
         copy(0, i, piece(lax.rem(y + i + 1, 8)), along_y.at[y], peer).start()
     along_y[y] = tiles[m * GROUPS + jnp.minimum(y, GROUPS - 1)]
 
-    wide[...] = ens_ref[...].astype(jnp.float32)
+    arrived[5].wait()
+    wide[...] = ens[...].astype(jnp.float32)
     for g in range(8):
         going[g] = wide[:, g, :].astype(jnp.bfloat16)
+
+    for b in range(batches, own):
+        pool[b] = jnp.zeros(pool.shape[1:], jnp.float32)
+        facts[b] = jnp.zeros(facts.shape[1:], jnp.float32)
+    pool[own] = prior[...]
+    facts[own] = fact
 
     def wait_recv(phase, i, src, dst, peer):
         copy(phase, i, src, dst, peer).wait_recv()
@@ -218,37 +385,7 @@
             facts[b, :, lane] = get(t // GROUPS, t % GROUPS)
 
     unpack(lambda p, q: every[p, q], 0)
-    post_ref[...] = prior_ref[...]
-    carry[...] = jnp.where(
-        lax.broadcasted_iota(jnp.int32, carry.shape, 0) == lax.broadcasted_iota(jnp.int32, carry.shape, 1), 1.0, 0.0
-    )
-
-    @pl.loop(0, batches)
-    def _(b):
-        priors = pool[b]
-        spread = priors - jnp.sum(priors, axis=0, keepdims=True) * (1.0 / MEMBERS)
-        turned[...] = spread.T * (1.0 / (MEMBERS - 1))
-        gap = target[b] - priors
-        fact = facts[b]
-        var, cos, sin = fact[0:1], fact[1:2], fact[2:3]
-        cosine[...] = jnp.broadcast_to(cos, (HALF, BATCH)).T
-        sine[...] = jnp.broadcast_to(sin, (HALF, BATCH)).T
-        st = turned[...]
-        row = lax.broadcasted_iota(jnp.int32, (BATCH, HALF), 0)
-        lane = lax.broadcasted_iota(jnp.int32, (BATCH, HALF), 1)
-
-        def weight(c, s):
-            return eighth(cosine[...] * c + sine[...] * s)
-
-        def system(t):
-            part = slice(t * HALF, t * HALF + HALF)
-            w = weight(cos[:, part], sin[:, part])
-            return w * dot(st, spread[:, part]) + jnp.where(row == lane + t * HALF, var[:, part], 0.0)
-
-        left, right = system(0), system(1)
-        a12 = right[:HALF]
-        half[0] = left[:HALF]
-
+    def spread_rest(b):
         @pl.when(b == 0)
         def _():
             for i, peer in enumerate(to_y):
@@ -258,12 +395,7 @@
                 copy(7, i, part, part, peer).start()
             copy(8, 0, part, part, there).start()
 
-        first = invert(half.at[0], board.at[0])
-        both = dot(jnp.concatenate([left[HALF:], gap[:, :HALF]], 0), first)
-        schur = jnp.concatenate([right[HALF:], gap[:, HALF:]], 0) - dot(both, a12)
-        half[1] = schur[:HALF]
-        second = invert(half.at[1], board.at[1])
-
+    def forward_rest(b):
         @pl.when(b == 0)
         def _():
             for i, peer in enumerate(to_x):
@@ -271,20 +403,7 @@
                 wait_recv(7, i, got, got, peer)
                 copy(8, i + 1, got, got, there).start()
 
-        x2 = dot(schur[HALF:], second)
-        x1 = both[HALF:] - dot(x2, both[:HALF])
-        solved = jnp.concatenate([x1, x2], 1)
-
-        def regress(field, c, s):
-            g = weight(c, s) * dot(st, field)
-            return field + dot(solved, g)
-
-        for t in range(2):
-            part = slice(t * HALF, t * HALF + HALF)
-            c, s = tiles[40 + t][1:2], tiles[40 + t][2:3]
-            post_ref[:, part] = regress(post_ref[:, part], c, s)
-        carry[...] = regress(carry[...], block_ref[0:1, :], block_ref[1:2, :])
-
+    def take_rest(b):
         @pl.when(b == 0)
         def _():
             wait_recv(8, 0, every_rest.at[m, used], every_rest.at[there[0], used], there)
@@ -301,13 +420,10 @@
             for g in range(8):
                 state[rows * g : rows * g + rows, :] = coming[g].astype(jnp.float32)
 
-        @pl.loop(b + 1, batches)
-        def _(k):
-            c = facts[k][1:2]
-            s = facts[k][2:3]
-            for t in range(2):
-                part = slice(t * HALF, t * HALF + HALF)
-                pool[k, :, part] = regress(pool[k, :, part], c[:, part], s[:, part])
+    last, fields = assimilate(
+        batches, pool, target, facts, carry, blockrow, turned, turned_low, cosine, sine, solved, gains, half, board,
+        (spread_rest, forward_rest, take_rest),
+    )
 
     for i, peer in enumerate(to_y):
         copy(0, i, tiles.at[0], along_y.at[y], peer).wait_send()
@@ -326,15 +442,21 @@
     for i, peer in enumerate(to_m):
         copy(9, i, going.at[0], coming.at[m], peer).wait_send()
 
-    final = carry[...][:, :MEMBERS]
+    for _ in later(last, fields[2:]):
+        pass
+    final = cat1(*split(carry[...][:, :MEMBERS], 3))
     for t in range(0, state.shape[1], BATCH):
         part = slice(t, t + BATCH)
-        state[:, part] = dot(final, state[:, part])
+        f = state[:, part].astype(jnp.bfloat16)
+        state[:, part] = once(final, cat0(f, f, f))
     for g in range(8):
         going[g] = state[rows * g : rows * g + rows, :].astype(jnp.bfloat16)
     for i, peer in enumerate(to_m):
         copy(10, i, going.at[lax.rem(m + i + 1, 8)], back.at[m], peer).start()
     back[m] = going[m]
+    for _ in later(last, fields[:2]):
+        pass
+    post_ref[...] = pool[own]
     for i, peer in enumerate(to_m):
         one = copy(10, i, going.at[0], back.at[lax.rem(m + 7 - i, 8)], peer)
         one.wait_recv()
@@ -345,15 +467,8 @@
 
 
 def shards(ensemble, obs_prior, obs_value, obs_var, obs_noise, obs_block, batch_owner):
-    columns_n = lax.axis_size("col")
-    column = lax.axis_index("col")
-    member = lax.axis_index("mem")
-    rows, blocks_own, cells = ensemble.shape
-    blocks = blocks_own * columns_n
+    rows, _, cells = ensemble.shape
     batches = batch_owner.shape[0]
-    angle = obs_block.astype(jnp.float32) * (math.pi / blocks)
-    block_angle = (column * blocks_own + member).astype(jnp.float32) * (math.pi / blocks)
-    blockrow = jnp.broadcast_to(jnp.stack([jnp.cos(block_angle), jnp.sin(block_angle)])[:, None], (2, HALF))
     vmem = pl.BlockSpec(memory_space=pltpu.VMEM)
     f32, bf16 = jnp.float32, jnp.bfloat16
     return pl.pallas_call(
@@ -362,9 +477,16 @@
             jax.ShapeDtypeStruct(ensemble.shape, bf16),
             jax.ShapeDtypeStruct(obs_prior.shape, f32),
         ),
-        in_specs=[vmem] * 7 + [pl.BlockSpec(memory_space=pltpu.SMEM)],
+        in_specs=[pl.BlockSpec(memory_space=pltpu.HBM)] * 6 + [pl.BlockSpec(memory_space=pltpu.SMEM)],
         out_specs=(vmem, vmem),
         scratch_shapes=[
+            pltpu.VMEM(ensemble.shape, bf16),
+            pltpu.VMEM(obs_prior.shape, f32),
+            pltpu.VMEM((1, BATCH), f32),
+            pltpu.VMEM((1, BATCH), f32),
+            pltpu.VMEM(obs_prior.shape, f32),
+            pltpu.VMEM((1, BATCH), jnp.int32),
+            pltpu.VMEM((8, HALF), f32),
             pltpu.VMEM((TILES, 8, HALF), f32),
             pltpu.VMEM((8, 8, HALF), f32),
             pltpu.VMEM((batches, 8, HALF), f32),
@@ -378,22 +500,26 @@
             pltpu.VMEM((8, rows, cells), bf16),
             pltpu.VMEM((8, rows, cells), bf16),
             pltpu.VMEM((MEMBERS, cells), f32),
+            pltpu.VMEM((2 * batches, MEMBERS, BATCH), f32),
             pltpu.VMEM((batches, MEMBERS, BATCH), f32),
-            pltpu.VMEM((batches, MEMBERS, BATCH), f32),
-            pltpu.VMEM((batches, 8, BATCH), f32),
+            pltpu.VMEM((2 * batches, 8, BATCH), f32),
             pltpu.VMEM((MEMBERS, HALF), f32),
-            pltpu.VMEM((BATCH, MEMBERS), f32),
-            pltpu.VMEM((BATCH, HALF), f32),
-            pltpu.VMEM((BATCH, HALF), f32),
+            pltpu.VMEM((2, BATCH, 3 * MEMBERS), bf16),
+            pltpu.VMEM((2, BATCH, 3 * MEMBERS), bf16),
+            pltpu.VMEM((2, BATCH, HALF), f32),
+            pltpu.VMEM((2, BATCH, HALF), f32),
+            pltpu.VMEM((2, 3 * MEMBERS, BATCH), bf16),
+            pltpu.VMEM((2, 3, BATCH, HALF), bf16),
             pltpu.VMEM((2, HALF, HALF), f32),
             pltpu.VMEM((2, 72 * HALF // 8, HALF), f32),
+            pltpu.SemaphoreType.DMA((6,)),
             pltpu.SemaphoreType.DMA((11, 7)),
             pltpu.SemaphoreType.DMA((11, 7)),
         ],
-        compiler_params=pltpu.CompilerParams(collective_id=0, has_side_effects=True, vmem_limit_bytes=48 << 20),
+        compiler_params=pltpu.CompilerParams(collective_id=0, has_side_effects=True, vmem_limit_bytes=63 << 20),
         name="regress_all",
     )(
-        ensemble, obs_prior, obs_value[None], obs_var[None], obs_noise, angle[None], blockrow, batch_owner
+        ensemble, obs_prior, obs_value[None], obs_var[None], obs_noise, obs_block[None], batch_owner
     )
 
 

time: 160 us -> 128 us (0.80)
  Pallas kernels: 154 us -> 124 us
  local copies, waits for them, and re-layouts: 5.36 us -> 2.26 us
    pallas_call x1, Pallas kernels: 154 us -> 124 us  [shards(): pl.pallas_call(regress_all, out_shape=(jax.ShapeDtypeStruct(ensemble.shap...]
    unnamed x16 -> x4, local copies, waits for them, and re-layouts: 5.29 us -> 2.26 us
where the time goes in v3:
time: 128 us; the launch traced here: 127 us
  Pallas kernels  124 us (97%)
  local copies, waits for them, and re-layouts  2.26 us (2%)
    pallas_call x1, Pallas kernels, shards(): pl.pallas_call(regress_all, out_shape=(jax.ShapeDtypeStruct(ensemble.shap...  124 us

profile of v3, /device:TPU:1, one launch (start us, length us, event | category | flops | bytes accessed | tf_op | source)
XLA Modules:
  0.0 127.4 jit_solution(9019582289062218499)
XLA Ops:
  0.6 124.5 %regress_all.1 = (bf16[10,8,1024]{2,1,0:T(8,128)(2,1)}, f32[80,256]{1,0:T(8,128)}) custom-call(bf16[10,8,1024]{2,1,0:T(8,128)(2,1)} %ens_hbm.1, f32[80,256]{1,0:T(8,128)} %prior_hbm.1, f32[1,256]{1,0:T(1,128)} %bitcast.3, f32[1,256]{1,0:T(1,128)} %bitcast.4, f32[80,256]{1,0:T(8,128)} %noise_hbm.1, s32[1,256]{1,0:T(1,128)} %bitcast.5, s32[8]{0:T(128)} %owner_ref.1), custom_call_target="tpu_custom_call" | custom-call | tf_op jit(solution)/shard_map/regress_all/pallas_call | solution.py:474
  125.1 0.0 copy-start
  125.1 1.6 %copy.11 = bf16[10,8,1024]{2,1,0:T(8,128)(2,1)} copy(bf16[10,8,1024]{2,1,0:T(8,128)(2,1)} %get-tuple-element.4) | data formatting | bytes 327680
  126.8 0.0 copy-done
  126.8 0.6 copy.12
Async XLA Ops:
  125.1 1.6 %copy-start = (f32[80,256]{1,0:T(8,128)S(1)}, f32[80,256]{1,0:T(8,128)}, u32[]{:S(2)}) copy-start(f32[80,256]{1,0:T(8,128)} %get-tuple-element.5) | copy-start | bytes 245764

commit v4 on v3

--- a/solution.py
+++ b/solution.py
@@ -14,6 +14,7 @@
 HALF = 128
 GROUPS = 6
 TILES = 8 * GROUPS
+LEAD = 2
 
 
 def split(x, n):
@@ -224,10 +225,10 @@
         both = narrow(cat0(left[HALF:], gap[:, :HALF]), first)
         schur = cat0(right[HALF:], gap[:, HALF:]) - narrow(both, a12)
         half[1] = schur[:HALF]
+        hooks[1](b)
         second = invert(half.at[1], board.at[1], between)
         for _ in steps:
             pass
-        hooks[1](b)
         x2 = narrow(schur[HALF:], second)
         x1 = both[HALF:] - narrow(x2, both[:HALF])
         solved[now] = cat0(*split(cat1(x1, x2), 3))
@@ -331,34 +332,27 @@
     owners = [owner_ref[j] for j in range(batches)]
     for j in range(batches):
         picked[j] = along_y[lax.rem(owners[j], 8)]
-    rest = pl.ds(1, batches - 1)
+    lead, rest = pl.ds(0, LEAD), pl.ds(LEAD, batches - LEAD)
     for i, peer in enumerate(to_z):
-        copy(1, i, picked.at[0], along_z.at[z], peer).start()
+        copy(1, i, picked.at[lead], along_z.at[z], peer).start()
     for i, peer in enumerate(to_z):
         copy(2, i, picked.at[rest], along_z_rest.at[z], peer).start()
-    along_z[z] = picked[0]
-    along_z_rest[z] = picked[1:]
+    along_z[z] = picked[:LEAD]
+    along_z_rest[z] = picked[LEAD:]
     for i, peer in enumerate(to_z):
-        wait_recv(1, i, picked.at[0], along_z.at[lax.rem(z + 7 - i, 8)], peer)
-    chosen[0] = along_z[owners[0] // 8]
+        wait_recv(1, i, picked.at[lead], along_z.at[lax.rem(z + 7 - i, 8)], peer)
+    for j in range(LEAD):
+        chosen[j] = along_z[owners[j] // 8, j]
     for i, peer in enumerate(to_y):
-        copy(3, i, chosen.at[0], every.at[m, y], peer).start()
-    every[m, y] = chosen[0]
+        copy(3, i, chosen.at[lead], every.at[m, y], peer).start()
+    every[m, y] = chosen[:LEAD]
     for i, peer in enumerate(to_y):
-        wait_recv(3, i, chosen.at[0], every.at[m, lax.rem(y + 7 - i, 8)], peer)
+        wait_recv(3, i, chosen.at[lead], every.at[m, lax.rem(y + 7 - i, 8)], peer)
     used = pl.ds(0, GROUPS)
     mine = every.at[m, used]
     for i, peer in enumerate(to_x):
         copy(4, i, mine, mine, peer).start()
     copy(5, 0, mine, mine, there).start()
-
-    for i, peer in enumerate(to_z):
-        wait_recv(2, i, picked.at[rest], along_z_rest.at[lax.rem(z + 7 - i, 8)], peer)
-    for j in range(1, batches):
-        chosen[j] = along_z_rest[owners[j] // 8, j - 1]
-    for i, peer in enumerate(to_y):
-        copy(6, i, chosen.at[rest], every_rest.at[m, y], peer).start()
-    every_rest[m, y] = chosen[1:]
 
     def source(i):
         return lax.rem(x + 3 - i, 4) * 2
@@ -384,7 +378,19 @@
             lane = slice(t % 2 * HALF, t % 2 * HALF + HALF)
             facts[b, :, lane] = get(t // GROUPS, t % GROUPS)
 
-    unpack(lambda p, q: every[p, q], 0)
+    for j in range(LEAD):
+        unpack(lambda p, q: every[p, q, j], j)
+    def pick_rest(b):
+        @pl.when(b == 0)
+        def _():
+            for i, peer in enumerate(to_z):
+                wait_recv(2, i, picked.at[rest], along_z_rest.at[lax.rem(z + 7 - i, 8)], peer)
+            for j in range(LEAD, batches):
+                chosen[j] = along_z_rest[owners[j] // 8, j - LEAD]
+            for i, peer in enumerate(to_y):
+                copy(6, i, chosen.at[rest], every_rest.at[m, y], peer).start()
+            every_rest[m, y] = chosen[LEAD:]
+
     def spread_rest(b):
         @pl.when(b == 0)
         def _():
@@ -404,16 +410,16 @@
                 copy(8, i + 1, got, got, there).start()
 
     def take_rest(b):
-        @pl.when(b == 0)
+        @pl.when(b == LEAD - 1)
         def _():
             wait_recv(8, 0, every_rest.at[m, used], every_rest.at[there[0], used], there)
             for i, peer in enumerate(to_x):
                 got = every_rest.at[source(i) + 1 - core, used]
                 wait_recv(8, i + 1, got, got, there)
 
-            @pl.loop(1, batches)
+            @pl.loop(LEAD, batches)
             def _(k):
-                unpack(lambda p, q: every_rest[p, q, k - 1], k)
+                unpack(lambda p, q: every_rest[p, q, k - LEAD], k)
 
             for i, peer in enumerate(to_m):
                 wait_recv(9, i, going.at[0], coming.at[lax.rem(m + 7 - i, 8)], peer)
@@ -422,15 +428,15 @@
 
     last, fields = assimilate(
         batches, pool, target, facts, carry, blockrow, turned, turned_low, cosine, sine, solved, gains, half, board,
-        (spread_rest, forward_rest, take_rest),
+        (lambda b: (pick_rest(b), take_rest(b)), spread_rest, forward_rest),
     )
 
     for i, peer in enumerate(to_y):
         copy(0, i, tiles.at[0], along_y.at[y], peer).wait_send()
-        copy(3, i, chosen.at[0], every.at[m, y], peer).wait_send()
+        copy(3, i, chosen.at[lead], every.at[m, y], peer).wait_send()
         copy(6, i, chosen.at[rest], every_rest.at[m, y], peer).wait_send()
     for i, peer in enumerate(to_z):
-        copy(1, i, picked.at[0], along_z.at[z], peer).wait_send()
+        copy(1, i, picked.at[lead], along_z.at[z], peer).wait_send()
         copy(2, i, picked.at[rest], along_z_rest.at[z], peer).wait_send()
     part = every_rest.at[m, used]
     for i, peer in enumerate(to_x):
@@ -490,11 +496,11 @@
             pltpu.VMEM((TILES, 8, HALF), f32),
             pltpu.VMEM((8, 8, HALF), f32),
             pltpu.VMEM((batches, 8, HALF), f32),
-            pltpu.VMEM((8, 8, HALF), f32),
-            pltpu.VMEM((8, batches - 1, 8, HALF), f32),
+            pltpu.VMEM((8, LEAD, 8, HALF), f32),
+            pltpu.VMEM((8, batches - LEAD, 8, HALF), f32),
             pltpu.VMEM((batches, 8, HALF), f32),
-            pltpu.VMEM((8, 8, 8, HALF), f32),
-            pltpu.VMEM((8, 8, batches - 1, 8, HALF), f32),
+            pltpu.VMEM((8, 8, LEAD, 8, HALF), f32),
+            pltpu.VMEM((8, 8, batches - LEAD, 8, HALF), f32),
             pltpu.VMEM(ensemble.shape, f32),
             pltpu.VMEM((8, rows, cells), bf16),
             pltpu.VMEM((8, rows, cells), bf16),

time: 128 us -> 133 us (1.039)
  Pallas kernels: 124 us -> 130 us
    pallas_call x1, Pallas kernels: 124 us -> 130 us  [shards(): pl.pallas_call(regress_all, out_shape=(jax.ShapeDtypeStruct(ensemble.shap...]
where the time goes in v4:
time: 133 us
  Pallas kernels  130 us (98%)
  local copies, waits for them, and re-layouts  2.26 us (2%)
    pallas_call x1, Pallas kernels, shards(): pl.pallas_call(regress_all, out_shape=(jax.ShapeDtypeStruct(ensemble.shap...  130 us

profile of v4, /device:TPU:1, one launch (start us, length us, event | category | flops | bytes accessed | tf_op | source)
XLA Modules:
  0.0 132.9 jit_solution(3028430846747120840)
XLA Ops:
  0.6 130.0 %regress_all.1 = (bf16[10,8,1024]{2,1,0:T(8,128)(2,1)}, f32[80,256]{1,0:T(8,128)}) custom-call(bf16[10,8,1024]{2,1,0:T(8,128)(2,1)} %ens_hbm.1, f32[80,256]{1,0:T(8,128)} %prior_hbm.1, f32[1,256]{1,0:T(1,128)} %bitcast.3, f32[1,256]{1,0:T(1,128)} %bitcast.4, f32[80,256]{1,0:T(8,128)} %noise_hbm.1, s32[1,256]{1,0:T(1,128)} %bitcast.5, s32[8]{0:T(128)} %owner_ref.1), custom_call_target="tpu_custom_call" | custom-call | tf_op jit(solution)/shard_map/regress_all/pallas_call | solution.py:480
  130.7 0.0 copy-start
  130.7 1.6 %copy.11 = bf16[10,8,1024]{2,1,0:T(8,128)(2,1)} copy(bf16[10,8,1024]{2,1,0:T(8,128)(2,1)} %get-tuple-element.4) | data formatting | bytes 327680
  132.3 0.0 copy-done
  132.3 0.6 copy.12
Async XLA Ops:
  130.7 1.6 %copy-start = (f32[80,256]{1,0:T(8,128)S(1)}, f32[80,256]{1,0:T(8,128)}, u32[]{:S(2)}) copy-start(f32[80,256]{1,0:T(8,128)} %get-tuple-element.5) | copy-start | bytes 245764
